TPU v7x, 32 devices: a whole 2x2x4 slice. The times are simulated.
32 devices in a mesh: grp: 2 (over y), row: 4 (over z), col: 2 (over x), rep: 2 (over core).
Axes of the slice: x: 2, y: 2, z: 4, core: 2. Of those that a mesh axis runs over, the one named last changes fastest.
Arguments:
- integrals: bfloat16 [32, 1024, 1024], P(('grp', 'rep'), 'row', 'col'), parts along dimension 0, may hold values from -0.078125 to 0.078125
- density: bfloat16 [2048, 1024], P(('grp', 'row', 'col')), parts along dimension 0, may hold values from -6 to 6
- tile_mask: int32 [4, 16, 16], P(('grp', 'rep'), 'row', 'col'), parts along dimension 0, may hold values 0 or 1
Outputs:
- exchange: bfloat16 [2048, 1024], P(('grp', 'row', 'col', 'rep')), parts along dimension 0
There are 2 independent parts, one for each index of `grp`. A program takes and returns all parts, laid end to end along the dimension named above; each array names one. Nothing has to cross between parts.
All inputs are finite; a program needn't handle non-finite values. No bound on the sum of `tile_mask` on one device may be relied on, other than what follows from the above.
Results may differ from a plain program's by a relative error of at most 0.0049.
Values may be sent and summed in bfloat16 or wider, within the bound.
A program may use at most 64 MiB of HBM per device.

v0:
```python
import jax
import jax.numpy as jnp
from jax import lax
from jax.sharding import PartitionSpec as P


def shards(integrals, density, tile_mask):
    aux_rows, ao_rows, ao_cols = integrals.shape
    mask_aux, mask_rows, mask_cols = tile_mask.shape
    shaped = integrals.reshape(
        mask_aux,
        aux_rows // mask_aux,
        mask_rows,
        ao_rows // mask_rows,
        mask_cols,
        ao_cols // mask_cols,
    )
    weights = tile_mask.astype(jnp.bfloat16)[:, None, :, None, :, None]
    screened = (shaped * weights).reshape(aux_rows, ao_rows, ao_cols)
    owned = lax.all_to_all(
        lax.all_to_all(screened, "row", split_axis=0, concat_axis=1, tiled=True),
        "col",
        split_axis=0,
        concat_axis=2,
        tiled=True,
    )
    full_density = lax.all_gather(density, ("row", "col"), axis=0, tiled=True)
    half = jnp.einsum(
        "amn,ns->ams", owned, full_density, preferred_element_type=jnp.float32
    ).astype(jnp.bfloat16)
    result = lax.psum_scatter(
        jnp.einsum("ams,als->ml", half, owned, preferred_element_type=jnp.float32),
        ("row", "col", "rep"),
        scatter_dimension=0,
        tiled=True,
    )
    return result.astype(jnp.bfloat16)


def solution(mesh):
    placed = (
        P(("grp", "rep"), "row", "col"),
        P(("grp", "row", "col"), None),
        P(("grp", "rep"), "row", "col"),
    )
    return jax.shard_map(
        shards,
        mesh=mesh,
        in_specs=placed,
        out_specs=P(("grp", "row", "col", "rep"), None),
        check_vma=False,
    )
```

profile of v0, /device:TPU:0, one launch (start us, length us, event | category | flops | bytes accessed | tf_op | source)
XLA Modules:
  0.0 200.3 jit_solution(8325474043487297083)
XLA Ops:
  6.5 0.7 convert_bitcast_fusion
  7.2 0.1 mul.18
  7.4 0.3 mul.19
  7.7 3.1 %broadcast_multiply_fusion = bf16[8,256,512]{2,1,0:T(8,128)(2,1)} fusion(bf16[8,256,512]{2,1,0:T(8,128)(2,1)} %param.3, bf16[256,512]{1,0:T(8,128)(2,1)S(1)} %mul.19), kind=kLoop, calls=%fused_computation.3 | loop fusion | flops 1048576 | bytes 4456448 | tf_op jit(solution)/shard_map/mul | solution.py:19
  10.8 6.3 %all-to-all-start = ((bf16[8,256,512]{2,1,0:T(8,128)(2,1)}), bf16[8,256,512]{2,1,0:T(8,128)(2,1)S(1)}, u32[]{:S(2)}, u32[]{:S(2)}) async-start(bf16[8,256,512]{2,1,0:T(8,128)(2,1)} %broadcast_multiply_fusion), calls=%async_computation | async-start | bytes 4194304 | tf_op jit(solution)/shard_map/all_to_all | solution.py:21
  17.1 0.0 all-gather.2.cloned.1.call-start
  17.1 0.7 all-gather.2.cloned.1.call-update
  17.9 0.0 reduce-scatter.2.cloned.1.call-start
  17.9 55.9 %all-to-all-done = bf16[8,256,512]{2,1,0:T(8,128)(2,1)S(1)} async-done(((bf16[8,256,512]{2,1,0:T(8,128)(2,1)}), bf16[8,256,512]{2,1,0:T(8,128)(2,1)S(1)}, u32[]{:S(2)}, u32[]{:S(2)}) %all-to-all-start) | async-done | bytes 2097184 | tf_op jit(solution)/shard_map/all_to_all | solution.py:21
  73.8 0.2 copy.5
  74.0 33.3 %all_to_all.33 = bf16[2,1024,512]{2,1,0:T(8,128)(2,1)S(1)} all-to-all(bf16[2,1024,512]{2,1,0:T(8,128)(2,1)S(1)} %bitcast.16), channel_id=1, replica_groups=mesh['grp'=2,'row'=4,'col'=2,'rep'=2] {'col'}, dimensions={0} | all-to-all | bytes 4194304 | tf_op jit(solution)/shard_map/all_to_all | solution.py:20
  107.3 2.4 %copy.6 = bf16[1,1024,2,512]{1,3,2,0:T(8,128)(2,1)} copy(bf16[1,1024,2,512]{3,1,2,0:T(8,128)(2,1)S(1)} %bitcast.17) | data formatting | bytes 4194304 | tf_op jit(solution)/shard_map/all_to_all | solution.py:20
  109.7 0.0 all-gather.2.cloned.1.call-done
  109.7 9.3 %fusion = f32[1024,1024]{1,0:T(8,128)} fusion(bf16[1024,1024]{0,1:T(8,128)(2,1)} %bitcast.18, bf16[1024,1024]{1,0:T(8,128)(2,1)} %all-gather.2.cloned.1.call-done), kind=kOutput, calls=%fused_computation | convolution fusion | flops 4296015872 | bytes 8388608 | tf_op jit(solution)/shard_map/ams,als->ml/dot_general | solution.py:32
  119.1 0.0 reduce-scatter.2.cloned.1.call-update
  119.1 72.8 %reduce-scatter.2.cloned.1.call-done = f32[64,1024]{1,0:T(8,128)} async-done(((f32[1024,1024]{1,0:T(8,128)}), f32[64,1024]{1,0:T(8,128)}) %reduce-scatter.2.cloned.1.call-update) | async-done | bytes 262160 | tf_op jit(solution)/shard_map/reduce_scatter | solution.py:31
  191.9 1.6 convert_element_type.12
Async XLA Ops:
  10.8 63.0 %all-to-all-start = ((bf16[8,256,512]{2,1,0:T(8,128)(2,1)}), bf16[8,256,512]{2,1,0:T(8,128)(2,1)S(1)}, u32[]{:S(2)}, u32[]{:S(2)}) async-start(bf16[8,256,512]{2,1,0:T(8,128)(2,1)} %broadcast_multiply_fusion), calls=%async_computation | async-start | bytes 4194304 | tf_op jit(solution)/shard_map/all_to_all | solution.py:21
  17.1 92.6 %all-gather.2.cloned.1.call-start = ((), (), s32[]{:S(2)}) async-start(), calls=%async_computation.3 | async-start | bytes 2359296 | tf_op jit(solution)/shard_map/all_gather | solution.py:27
  17.9 174.0 %reduce-scatter.2.cloned.1.call-start = ((), (), s32[]{:S(2)}) async-start(), calls=%async_computation.4 | async-start | bytes 4456448 | tf_op jit(solution)/shard_map/reduce_scatter | solution.py:31
Sparse Core Ops, SparseCore 0:
  20.1 82.7 all-gather.1
  119.2 72.6 reduce-scatter.1
where the time goes:
time: 201 us; the launch traced here: 200 us
  waiting for transfers between devices  129 us (64%)
  blocking collectives  33.3 us (17%)
  between operations  13.4 us (7%)
  matrix products  9.34 us (5%)
  starting transfers between devices  6.36 us (3%)
  other arithmetic  5.43 us (3%)
  local copies, waits for them, and re-layouts  3.12 us (2%)
    reduce_scatter x1, waiting for transfers between devices, shards(): lax.psum_scatter(jnp.einsum('ams,als->ml', half, owned, preferred_element...  72.8 us
    all_to_all x1, waiting for transfers between devices, shards(): lax.all_to_all(screened, 'row', split_axis=0, concat_axis=1, tiled=True)  55.9 us
    all_to_all x1, blocking collectives, shards(): lax.all_to_all(lax.all_to_all(screened, 'row', split_axis=0, concat_axis=...  33.3 us
    dot_general x1, matrix products, shards(): jnp.einsum('ams,als->ml', half, owned, preferred_element_type=jnp.float32)  9.34 us
    all_to_all x1, starting transfers between devices, shards(): lax.all_to_all(screened, 'row', split_axis=0, concat_axis=1, tiled=True)  6.32 us
  transfers between devices with their start and end apart: 3, of which 2 were waited for; matrix products, arithmetic and copies ran while one was open for 1% of the time, Pallas kernels for 0%

commit v1 on v0

--- a/solution.py
+++ b/solution.py
@@ -1,10 +1,216 @@
+import functools
+
 import jax
 import jax.numpy as jnp
 from jax import lax
+from jax.experimental import pallas as pl
+from jax.experimental.pallas import tpu as pltpu
 from jax.sharding import PartitionSpec as P
 
-
-def shards(integrals, density, tile_mask):
+F32 = jnp.float32
+BF16 = jnp.bfloat16
+
+
+def exchange_kernel(
+    x_ref, d_ref, mask_ref, out_ref,
+    sbuf, owned, dens, half, kf, ks, crecv, xs, xrecv, zs, zrecv, tot,
+    a_send, a_recv, dz_send, dz_recv, dx_send, dx_recv, dc_send, dc_recv,
+    kc_send, kc_recv, kx_send, kx_recv, kz_send, kz_recv,
+):
+    r, c, q = lax.axis_index("row"), lax.axis_index("col"), lax.axis_index("rep")
+    hi, lo = r // 2, r % 2
+    far = [r, hi * 2 + 1 - lo, (1 - hi) * 2 + lo, 3 - r]
+    oc, oq = 1 - c, 1 - q
+    me = 2 * r + c
+
+    def dev(row, col, rep):
+        return {"row": row, "col": col, "rep": rep}
+
+    sends = []
+
+    def copy(src, dst, ssem, rsem, to):
+        return pltpu.make_async_remote_copy(
+            src_ref=src, dst_ref=dst, send_sem=ssem, recv_sem=rsem,
+            device_id=to, device_id_type=pl.DeviceIdType.MESH,
+        )
+
+    def send(src, dst, ssem, rsem, to):
+        made = copy(src, dst, ssem, rsem, to)
+        made.start()
+        sends.append(made)
+
+    def arrive(dst, ssem, rsem):
+        copy(dst, dst, ssem, rsem, dev(r, c, oq)).wait_recv()
+
+    barrier = pltpu.get_barrier_semaphore()
+    partners = [dev(r, c, oq), dev(r, oc, q)]
+    for k in (1, 2, 3):
+        partners += [dev(far[k], c, q), dev(far[k], oc, q)]
+    for to in partners:
+        pl.semaphore_signal(barrier, inc=1, device_id=to, device_id_type=pl.DeviceIdType.MESH)
+
+    rows, cols = x_ref.shape[1], x_ref.shape[2]
+    tiles_m, tiles_n = mask_ref.shape[1], mask_ref.shape[2]
+    tile_m, tile_n = rows // tiles_m, cols // tiles_n
+    lane = lax.broadcasted_iota(jnp.int32, (16, cols), 1) // tile_n
+    weights = []
+    for i in range(tiles_m):
+        line = jnp.zeros((16, cols), F32)
+        for j in range(tiles_n):
+            line = jnp.where(lane == j, mask_ref[0, i, j].astype(F32), line)
+        weights.append(line.astype(BF16)[None])
+
+    def screen(f, dst, at):
+        for i in range(tiles_m):
+            part = x_ref[f, pl.ds(i * tile_m, tile_m), :].reshape(tile_m // 16, 16, cols)
+            dst[at, pl.ds(i * tile_m, tile_m), :] = (part * weights[i]).reshape(tile_m, cols)
+
+    hd = d_ref.shape[0] // 2
+    for b in range(2):
+        dens[2 * me + b] = d_ref[pl.ds(b * hd, hd), :]
+
+    pl.semaphore_wait(barrier, len(partners))
+
+    mine = 2 * me + q
+    for k in (3, 2, 1):
+        send(dens.at[mine], dens.at[mine], dz_send.at[k], dz_recv.at[k], dev(far[k], c, q))
+    send(dens.at[mine], dens.at[mine], dx_send.at[0], dx_recv.at[0], dev(r, oc, q))
+
+    for k in (3, 2, 0, 1):
+        for cc in ((oc,) if k == 0 else (c, oc)):
+            f = 2 * far[k] + cc
+            screen(f, sbuf, f)
+            send(sbuf.at[f], owned.at[me], a_send.at[f], a_recv.at[me], dev(far[k], cc, q))
+    screen(me, owned, me)
+
+    for k in (1, 2, 3):
+        b = 2 * (2 * far[k] + c) + q
+        arrive(dens.at[b], dz_send.at[k], dz_recv.at[k])
+        send(dens.at[b], dens.at[b], dx_send.at[k], dx_recv.at[k], dev(r, oc, q))
+        send(dens.at[b], dens.at[b], dc_send.at[k], dc_recv.at[k], dev(r, c, oq))
+    for k in (0, 1, 2, 3):
+        b = 2 * (2 * far[k] + oc) + q
+        arrive(dens.at[b], dx_send.at[k], dx_recv.at[k])
+        send(dens.at[b], dens.at[b], dc_send.at[4 + k], dc_recv.at[4 + k], dev(r, c, oq))
+    for k in (1, 2, 3):
+        b = 2 * (2 * far[k] + c) + oq
+        arrive(dens.at[b], dc_send.at[k], dc_recv.at[k])
+    for k in (0, 1, 2, 3):
+        b = 2 * (2 * far[k] + oc) + oq
+        arrive(dens.at[b], dc_send.at[4 + k], dc_recv.at[4 + k])
+
+    n = d_ref.shape[1]
+    hb = dens.shape[0] // 2
+    gran = out_ref.shape[0]
+
+    def product(k, j):
+        acc = jnp.zeros((rows, rows), F32)
+        for cc in range(2):
+            acc += lax.dot_general(
+                half[k, :, pl.ds(cc * cols, cols)], owned[2 * far[j] + cc],
+                (((1,), (1,)), ((), ())), preferred_element_type=F32,
+            )
+        at = pl.ds(pl.multiple_of(far[j] * rows, rows), rows)
+        for c2 in range(2):
+            for q2 in range(2):
+                part = acc[(2 * c2 + q2) * gran:(2 * c2 + q2 + 1) * gran, :]
+                kf[k, q2, c2, :, at] = part
+                ks[k, q2, c2, :, at] = part.astype(BF16)
+
+    done = []
+    for k in (0, 1, 2, 3):
+        for cc in ((oc,) if k == 0 else (c, oc)):
+            b = 2 * far[k] + cc
+            arrive(owned.at[b], a_send.at[b], a_recv.at[b])
+        for s in range(0, n, 256):
+            acc = jnp.zeros((rows, 256), F32)
+            for cc in range(2):
+                block = dens[pl.ds(cc * hb, hb), :, pl.ds(s, 256)].reshape(cols, 256)
+                acc += jnp.dot(owned[2 * far[k] + cc], block, preferred_element_type=F32)
+            half[k, :, pl.ds(s, 256)] = acc.astype(BF16)
+        if k < 3:
+            product(k, k)
+            for j in done:
+                product(k, j)
+                product(j, k)
+            done.append(k)
+
+    order = (3, 2, 1, 0)
+
+    def stage_a(k):
+        for j in ((0, 1, 2, 3) if k == 3 else (3,)):
+            product(k, j)
+        send(ks.at[k, oq], crecv.at[k], kc_send.at[k], kc_recv.at[k], dev(r, c, oq))
+
+    def stage_b(k):
+        arrive(crecv.at[k], kc_send.at[k], kc_recv.at[k])
+        xs[k] = (kf[k, q, oc] + crecv[k, oc].astype(F32)).astype(BF16)
+        send(xs.at[k], xrecv.at[k], kx_send.at[k], kx_recv.at[k], dev(r, oc, q))
+
+    def stage_c(k):
+        arrive(xrecv.at[k], kx_send.at[k], kx_recv.at[k])
+        total = kf[k, q, c] + crecv[k, c].astype(F32) + xrecv[k].astype(F32)
+        if k:
+            zs[k] = total.astype(BF16)
+            send(zs.at[k], zrecv.at[k], kz_send.at[k], kz_recv.at[k], dev(far[k], c, q))
+        else:
+            tot[...] = total
+
+    for t in range(6):
+        if t < 4:
+            stage_a(order[t])
+        if 0 <= t - 1 < 4:
+            stage_b(order[t - 1])
+        if 0 <= t - 2 < 4:
+            stage_c(order[t - 2])
+    total = tot[...]
+    for k in (1, 2, 3):
+        arrive(zrecv.at[k], kz_send.at[k], kz_recv.at[k])
+        total += zrecv[k].astype(F32)
+    out_ref[...] = total.astype(out_ref.dtype)
+    for made in sends:
+        made.wait_send()
+
+
+def fused(integrals, density, tile_mask, gran):
+    fns, rows, cols = integrals.shape
+    drows, n = density.shape
+    dma = pltpu.SemaphoreType.DMA
+    vmem = pltpu.VMEM
+    flops = 4 * n * n * n
+    return pl.pallas_call(
+        exchange_kernel,
+        out_shape=jax.ShapeDtypeStruct((gran, n), BF16),
+        in_specs=[
+            pl.BlockSpec(memory_space=pltpu.VMEM),
+            pl.BlockSpec(memory_space=pltpu.VMEM),
+            pl.BlockSpec(memory_space=pltpu.SMEM),
+        ],
+        out_specs=pl.BlockSpec(memory_space=pltpu.VMEM),
+        scratch_shapes=[
+            vmem((fns, rows, cols), BF16),
+            vmem((fns, rows, cols), BF16),
+            vmem((16, drows // 2, n), BF16),
+            vmem((4, rows, n), BF16),
+            vmem((4, 2, 2, gran, n), F32),
+            vmem((4, 2, 2, gran, n), BF16),
+            vmem((4, 2, gran, n), BF16),
+            vmem((4, gran, n), BF16),
+            vmem((4, gran, n), BF16),
+            vmem((4, gran, n), BF16),
+            vmem((4, gran, n), BF16),
+            vmem((gran, n), F32),
+            dma((8,)), dma((8,)), dma((4,)), dma((4,)), dma((4,)), dma((4,)), dma((8,)), dma((8,)),
+            dma((4,)), dma((4,)), dma((4,)), dma((4,)), dma((4,)), dma((4,)),
+        ],
+        compiler_params=pltpu.CompilerParams(
+            collective_id=0, has_side_effects=True, vmem_limit_bytes=48 * 1024 * 1024
+        ),
+        cost_estimate=pl.CostEstimate(flops=flops, bytes_accessed=5 * 1024 * 1024, transcendentals=0),
+    )(integrals, density, tile_mask)
+
+
+def general(integrals, density, tile_mask):
     aux_rows, ao_rows, ao_cols = integrals.shape
     mask_aux, mask_rows, mask_cols = tile_mask.shape
     shaped = integrals.reshape(
@@ -37,6 +243,25 @@
     return result.astype(jnp.bfloat16)
 
 
+def shards(mesh, integrals, density, tile_mask):
+    n_row, n_col, n_rep = (mesh.shape[name] for name in ("row", "col", "rep"))
+    fns, rows, cols = integrals.shape
+    gran = rows // (n_col * n_rep)
+    fits = (
+        (n_row, n_col, n_rep) == (4, 2, 2)
+        and fns == n_row * n_col
+        and tile_mask.shape[0] == 1
+        and gran % 16 == 0
+        and (rows // tile_mask.shape[1]) % 16 == 0
+        and rows % 128 == 0
+        and cols % 256 == 0
+        and density.shape[0] % 32 == 0
+    )
+    if fits:
+        return fused(integrals, density, tile_mask, gran)
+    return general(integrals, density, tile_mask)
+
+
 def solution(mesh):
     placed = (
         P(("grp", "rep"), "row", "col"),
@@ -44,7 +269,7 @@
         P(("grp", "rep"), "row", "col"),
     )
     return jax.shard_map(
-        shards,
+        functools.partial(shards, mesh),
         mesh=mesh,
         in_specs=placed,
         out_specs=P(("grp", "row", "col", "rep"), None),

time: 201 us -> 91 us (0.45)
  waiting for transfers between devices: 129 us -> 0 us
  Pallas kernels: 0 us -> 86.9 us
  blocking collectives: 33.3 us -> 0 us
  between operations: 13.4 us -> 0.01 us
  matrix products: 9.34 us -> 0 us
  starting transfers between devices: 6.36 us -> 0 us
  other arithmetic: 5.43 us -> 0 us
    pallas_call x0 -> x1, Pallas kernels: none -> 86.9 us  [fused(): pl.pallas_call(exchange_kernel, out_shape=jax.ShapeDtypeStruct((gran, n),...]
    reduce_scatter x1 -> x0, waiting for transfers between devices: 72.8 us -> none  [shards(): lax.psum_scatter(jnp.einsum('ams,als->ml', half, owned, preferred_element...]
    all_to_all x1 -> x0, waiting for transfers between devices: 55.9 us -> none  [shards(): lax.all_to_all(screened, 'row', split_axis=0, concat_axis=1, tiled=True)]
    all_to_all x1 -> x0, blocking collectives: 33.3 us -> none  [shards(): lax.all_to_all(lax.all_to_all(screened, 'row', split_axis=0, concat_axis=...]
    dot_general x1 -> x0, matrix products: 9.34 us -> none  [shards(): jnp.einsum('ams,als->ml', half, owned, preferred_element_type=jnp.float32)]
    all_to_all x1 -> x0, starting transfers between devices: 6.32 us -> none  [shards(): lax.all_to_all(screened, 'row', split_axis=0, concat_axis=1, tiled=True)]
    unnamed x0 -> x7, local copies, waits for them, and re-layouts: none -> 3.88 us
    mul x2 -> x0, other arithmetic: 3.81 us -> none  [shards(): screened = (shaped * weights).reshape(aux_rows, ao_rows, ao_cols)]
  transfers between devices with their start and end apart: 3 -> 0, of which waited for: 2 -> 0; matrix products, arithmetic and copies ran while one was open for 1% -> 0% of each run, Pallas kernels for 0% -> 0%
where the time goes in v1:
time: 91 us; the launch traced here: 90.8 us
  Pallas kernels  86.9 us (95%)
  local copies, waits for them, and re-layouts  3.88 us (4%)
    pallas_call x1, Pallas kernels, fused(): pl.pallas_call(exchange_kernel, out_shape=jax.ShapeDtypeStruct((gran, n),...  86.9 us
    unnamed x7, local copies, waits for them, and re-layouts  3.88 us

profile of v1, /device:TPU:0, one launch (start us, length us, event | category | flops | bytes accessed | tf_op | source)
XLA Modules:
  0.0 90.8 jit_solution(8350172699608331055)
XLA Ops:
  0.0 0.0 copy-start
  0.0 1.6 %copy-done = bf16[8,256,512]{2,1,0:T(8,128)(2,1)S(1)} copy-done((bf16[8,256,512]{2,1,0:T(8,128)(2,1)S(1)}, bf16[8,256,512]{2,1,0:T(8,128)(2,1)}, u32[]{:S(2)}) %copy-start) | copy-done | bytes 2097176
  1.6 0.0 copy-start.1
  1.6 0.9 %copy-done.1 = bf16[128,1024]{1,0:T(8,128)(2,1)S(1)} copy-done((bf16[128,1024]{1,0:T(8,128)(2,1)S(1)}, bf16[128,1024]{1,0:T(8,128)(2,1)}, u32[]{:S(2)}) %copy-start.1) | copy-done | bytes 262168
  2.5 0.0 copy-start.2
  2.5 0.7 copy-done.2
  3.2 86.9 %shard_map.37 = bf16[64,1024]{1,0:T(8,128)(2,1)S(1)} custom-call(bf16[8,256,512]{2,1,0:T(8,128)(2,1)S(1)} %copy-done, bf16[128,1024]{1,0:T(8,128)(2,1)S(1)} %copy-done.1, s32[1,4,8]{2,1,0:T(4,128)S(1)} %copy-done.2), custom_call_target="tpu_custom_call" | custom-call | flops 4294967296 | bytes 5242880 | tf_op jit(solution)/shard_map/pallas_call | solution.py:181
  90.1 0.7 copy.5
Async XLA Ops:
  0.0 1.6 %copy-start = (bf16[8,256,512]{2,1,0:T(8,128)(2,1)S(1)}, bf16[8,256,512]{2,1,0:T(8,128)(2,1)}, u32[]{:S(2)}) copy-start(bf16[8,256,512]{2,1,0:T(8,128)(2,1)} %x_ref.1) | copy-start | bytes 6291460
  1.6 0.9 %copy-start.1 = (bf16[128,1024]{1,0:T(8,128)(2,1)S(1)}, bf16[128,1024]{1,0:T(8,128)(2,1)}, u32[]{:S(2)}) copy-start(bf16[128,1024]{1,0:T(8,128)(2,1)} %d_ref.1) | copy-start | bytes 786436
  2.5 0.7 copy-start.2

commit v2 on v1

--- a/solution.py
+++ b/solution.py
@@ -9,12 +9,19 @@
 
 F32 = jnp.float32
 BF16 = jnp.bfloat16
+A2A_ORDER = ((2, 0), (2, 1), (1, 0), (0, 1), (1, 1), (3, 0), (3, 1))
+FIRST, SECOND = 2, 5
+ZFIRST = False
+
+
+EARLY = ((2, 0, 3), (1, 0, 3), (0, 0, 3))
+LATE = ((3, 0, 4), (2, 3, 1), (1, 3, 1), (0, 3, 1))
 
 
 def exchange_kernel(
-    x_ref, d_ref, mask_ref, out_ref,
-    sbuf, owned, dens, half, kf, ks, crecv, xs, xrecv, zs, zrecv, tot,
-    a_send, a_recv, dz_send, dz_recv, dx_send, dx_recv, dc_send, dc_recv,
+    x_hbm, d_hbm, mask_ref, out_ref,
+    x_ref, owned, dens, half, kf, ks, crecv, xs, xrecv, zs, zrecv, tot,
+    x_in, d_in, a_send, a_recv, dz_send, dz_recv, dx_send, dx_recv, dc_send, dc_recv,
     kc_send, kc_recv, kx_send, kx_recv, kz_send, kz_recv,
 ):
     r, c, q = lax.axis_index("row"), lax.axis_index("col"), lax.axis_index("rep")
@@ -48,6 +55,19 @@
         partners += [dev(far[k], c, q), dev(far[k], oc, q)]
     for to in partners:
         pl.semaphore_signal(barrier, inc=1, device_id=to, device_id_type=pl.DeviceIdType.MESH)
+
+    hd = d_hbm.shape[0] // 2
+    d_copies = [
+        pltpu.make_async_copy(d_hbm.at[pl.ds(b * hd, hd)], dens.at[2 * me + b], d_in.at[b]) for b in range(2)
+    ]
+    for made in d_copies:
+        made.start()
+    blocks = {(k, cc): 2 * far[k] + (c, oc)[cc] for k in range(4) for cc in range(2)}
+    x_copies = {}
+    for at in A2A_ORDER + ((0, 0),):
+        f = blocks[at]
+        x_copies[at] = pltpu.make_async_copy(x_hbm.at[f], x_ref.at[f], x_in.at[f])
+        x_copies[at].start()
 
     rows, cols = x_ref.shape[1], x_ref.shape[2]
     tiles_m, tiles_n = mask_ref.shape[1], mask_ref.shape[2]
@@ -60,38 +80,58 @@
             line = jnp.where(lane == j, mask_ref[0, i, j].astype(F32), line)
         weights.append(line.astype(BF16)[None])
 
-    def screen(f, dst, at):
+    def screen(at, dst, place):
+        f = blocks[at]
+        x_copies[at].wait()
         for i in range(tiles_m):
             part = x_ref[f, pl.ds(i * tile_m, tile_m), :].reshape(tile_m // 16, 16, cols)
-            dst[at, pl.ds(i * tile_m, tile_m), :] = (part * weights[i]).reshape(tile_m, cols)
-
-    hd = d_ref.shape[0] // 2
-    for b in range(2):
-        dens[2 * me + b] = d_ref[pl.ds(b * hd, hd), :]
-
+            dst[place, pl.ds(i * tile_m, tile_m), :] = (part * weights[i]).reshape(tile_m, cols)
+
+    ready = set()
+
+    def to_owner(at):
+        f = blocks[at]
+        if at not in ready:
+            screen(at, x_ref, f)
+            ready.add(at)
+        send(x_ref.at[f], owned.at[me], a_send.at[f], a_recv.at[me], dev(far[at[0]], (c, oc)[at[1]], q))
+
+    for made in d_copies:
+        made.wait()
+    screen(A2A_ORDER[0], x_ref, blocks[A2A_ORDER[0]])
+    ready.add(A2A_ORDER[0])
     pl.semaphore_wait(barrier, len(partners))
 
     mine = 2 * me + q
-    for k in (3, 2, 1):
+    for k in (2, 1):
         send(dens.at[mine], dens.at[mine], dz_send.at[k], dz_recv.at[k], dev(far[k], c, q))
     send(dens.at[mine], dens.at[mine], dx_send.at[0], dx_recv.at[0], dev(r, oc, q))
-
-    for k in (3, 2, 0, 1):
-        for cc in ((oc,) if k == 0 else (c, oc)):
-            f = 2 * far[k] + cc
-            screen(f, sbuf, f)
-            send(sbuf.at[f], owned.at[me], a_send.at[f], a_recv.at[me], dev(far[k], cc, q))
-    screen(me, owned, me)
-
-    for k in (1, 2, 3):
+    for at in A2A_ORDER[:FIRST]:
+        to_owner(at)
+    screen((0, 0), owned, me)
+
+    def dens_z(k):
         b = 2 * (2 * far[k] + c) + q
         arrive(dens.at[b], dz_send.at[k], dz_recv.at[k])
+        if k == 2:
+            send(dens.at[b], dens.at[b], dz_send.at[3], dz_recv.at[3], dev(far[1], c, q))
         send(dens.at[b], dens.at[b], dx_send.at[k], dx_recv.at[k], dev(r, oc, q))
         send(dens.at[b], dens.at[b], dc_send.at[k], dc_recv.at[k], dev(r, c, oq))
-    for k in (0, 1, 2, 3):
+
+    def dens_x(k):
         b = 2 * (2 * far[k] + oc) + q
         arrive(dens.at[b], dx_send.at[k], dx_recv.at[k])
         send(dens.at[b], dens.at[b], dc_send.at[4 + k], dc_recv.at[4 + k], dev(r, c, oq))
+
+    dens_z(1)
+    dens_z(2)
+    for at in A2A_ORDER[FIRST:SECOND]:
+        to_owner(at)
+    dens_z(3)
+    for at in A2A_ORDER[SECOND:]:
+        to_owner(at)
+    for k in (0, 1, 2, 3):
+        dens_x(k)
     for k in (1, 2, 3):
         b = 2 * (2 * far[k] + c) + oq
         arrive(dens.at[b], dc_send.at[k], dc_recv.at[k])
@@ -99,7 +139,7 @@
         b = 2 * (2 * far[k] + oc) + oq
         arrive(dens.at[b], dc_send.at[4 + k], dc_recv.at[4 + k])
 
-    n = d_ref.shape[1]
+    n = d_hbm.shape[1]
     hb = dens.shape[0] // 2
     gran = out_ref.shape[0]
 
@@ -110,17 +150,15 @@
                 half[k, :, pl.ds(cc * cols, cols)], owned[2 * far[j] + cc],
                 (((1,), (1,)), ((), ())), preferred_element_type=F32,
             )
-        at = pl.ds(pl.multiple_of(far[j] * rows, rows), rows)
         for c2 in range(2):
             for q2 in range(2):
                 part = acc[(2 * c2 + q2) * gran:(2 * c2 + q2 + 1) * gran, :]
-                kf[k, q2, c2, :, at] = part
-                ks[k, q2, c2, :, at] = part.astype(BF16)
-
-    done = []
-    for k in (0, 1, 2, 3):
-        for cc in ((oc,) if k == 0 else (c, oc)):
-            b = 2 * far[k] + cc
+                kf[k, q2, j, c2] = part
+                ks[k, q2, j, c2] = part.astype(BF16)
+
+    def row_block(k):
+        for cc in ((1,) if k == 0 else (0, 1)):
+            b = blocks[(k, cc)]
             arrive(owned.at[b], a_send.at[b], a_recv.at[b])
         for s in range(0, n, 256):
             acc = jnp.zeros((rows, 256), F32)
@@ -128,46 +166,68 @@
                 block = dens[pl.ds(cc * hb, hb), :, pl.ds(s, 256)].reshape(cols, 256)
                 acc += jnp.dot(owned[2 * far[k] + cc], block, preferred_element_type=F32)
             half[k, :, pl.ds(s, 256)] = acc.astype(BF16)
-        if k < 3:
-            product(k, k)
-            for j in done:
-                product(k, j)
-                product(j, k)
-            done.append(k)
-
-    order = (3, 2, 1, 0)
-
-    def stage_a(k):
-        for j in ((0, 1, 2, 3) if k == 3 else (3,)):
+
+    def place(item):
+        k, j, size = item
+        return (EARLY + LATE).index(item), k, pl.ds(j, size)
+
+    def over_core(item):
+        i, k, js = place(item)
+        send(ks.at[k, oq, js], crecv.at[k, js], kc_send.at[i], kc_recv.at[i], dev(r, c, oq))
+
+    def over_x(item):
+        i, k, js = place(item)
+        arrive(crecv.at[k, js], kc_send.at[i], kc_recv.at[i])
+        xs[k, js] = (kf[k, q, js, oc] + crecv[k, js, oc].astype(F32)).astype(BF16)
+        send(xs.at[k, js], xrecv.at[k, js], kx_send.at[i], kx_recv.at[i], dev(r, oc, q))
+
+    def over_z(item):
+        i, k, js = place(item)
+        arrive(xrecv.at[k, js], kx_send.at[i], kx_recv.at[i])
+        total = kf[k, q, js, c] + crecv[k, js, c].astype(F32) + xrecv[k, js].astype(F32)
+        if k:
+            zs[k, js] = total.astype(BF16)
+            send(zs.at[k, js], zrecv.at[k, js], kz_send.at[i], kz_recv.at[i], dev(far[k], c, q))
+        else:
+            tot[js] = total
+
+    for k in range(3):
+        row_block(k)
+        for j in range(k):
             product(k, j)
-        send(ks.at[k, oq], crecv.at[k], kc_send.at[k], kc_recv.at[k], dev(r, c, oq))
-
-    def stage_b(k):
-        arrive(crecv.at[k], kc_send.at[k], kc_recv.at[k])
-        xs[k] = (kf[k, q, oc] + crecv[k, oc].astype(F32)).astype(BF16)
-        send(xs.at[k], xrecv.at[k], kx_send.at[k], kx_recv.at[k], dev(r, oc, q))
-
-    def stage_c(k):
-        arrive(xrecv.at[k], kx_send.at[k], kx_recv.at[k])
-        total = kf[k, q, c] + crecv[k, c].astype(F32) + xrecv[k].astype(F32)
+            product(j, k)
+        product(k, k)
+    for item in EARLY:
+        over_core(item)
+    for item in EARLY:
+        over_x(item)
+    if ZFIRST:
+        for item in EARLY:
+            over_z(item)
+    row_block(3)
+    for j in range(4):
+        product(3, j)
+    over_core(LATE[0])
+    for k in (2, 1, 0):
+        product(k, 3)
+        over_core(LATE[3 - k])
+    if not ZFIRST:
+        for item in EARLY:
+            over_z(item)
+    for item in LATE:
+        over_x(item)
+    for item in LATE:
+        over_z(item)
+    for item in EARLY + LATE:
+        i, k, js = place(item)
         if k:
-            zs[k] = total.astype(BF16)
-            send(zs.at[k], zrecv.at[k], kz_send.at[k], kz_recv.at[k], dev(far[k], c, q))
-        else:
-            tot[...] = total
-
-    for t in range(6):
-        if t < 4:
-            stage_a(order[t])
-        if 0 <= t - 1 < 4:
-            stage_b(order[t - 1])
-        if 0 <= t - 2 < 4:
-            stage_c(order[t - 2])
-    total = tot[...]
-    for k in (1, 2, 3):
-        arrive(zrecv.at[k], kz_send.at[k], kz_recv.at[k])
-        total += zrecv[k].astype(F32)
-    out_ref[...] = total.astype(out_ref.dtype)
+            arrive(zrecv.at[k, js], kz_send.at[i], kz_recv.at[i])
+    for j in range(4):
+        total = tot[j]
+        for k in (1, 2, 3):
+            total += zrecv[k, k ^ j].astype(F32)
+        at = pl.ds(pl.multiple_of(far[j] * rows, rows), rows)
+        out_ref[:, at] = total.astype(out_ref.dtype)
     for made in sends:
         made.wait_send()
 
@@ -177,13 +237,12 @@
     drows, n = density.shape
     dma = pltpu.SemaphoreType.DMA
     vmem = pltpu.VMEM
-    flops = 4 * n * n * n
     return pl.pallas_call(
         exchange_kernel,
         out_shape=jax.ShapeDtypeStruct((gran, n), BF16),
         in_specs=[
-            pl.BlockSpec(memory_space=pltpu.VMEM),
-            pl.BlockSpec(memory_space=pltpu.VMEM),
+            pl.BlockSpec(memory_space=pl.ANY),
+            pl.BlockSpec(memory_space=pl.ANY),
             pl.BlockSpec(memory_space=pltpu.SMEM),
         ],
         out_specs=pl.BlockSpec(memory_space=pltpu.VMEM),
@@ -192,21 +251,21 @@
             vmem((fns, rows, cols), BF16),
             vmem((16, drows // 2, n), BF16),
             vmem((4, rows, n), BF16),
-            vmem((4, 2, 2, gran, n), F32),
-            vmem((4, 2, 2, gran, n), BF16),
-            vmem((4, 2, gran, n), BF16),
-            vmem((4, gran, n), BF16),
-            vmem((4, gran, n), BF16),
-            vmem((4, gran, n), BF16),
-            vmem((4, gran, n), BF16),
-            vmem((gran, n), F32),
-            dma((8,)), dma((8,)), dma((4,)), dma((4,)), dma((4,)), dma((4,)), dma((8,)), dma((8,)),
-            dma((4,)), dma((4,)), dma((4,)), dma((4,)), dma((4,)), dma((4,)),
+            vmem((4, 2, 4, 2, gran, rows), F32),
+            vmem((4, 2, 4, 2, gran, rows), BF16),
+            vmem((4, 4, 2, gran, rows), BF16),
+            vmem((4, 4, gran, rows), BF16),
+            vmem((4, 4, gran, rows), BF16),
+            vmem((4, 4, gran, rows), BF16),
+            vmem((4, 4, gran, rows), BF16),
+            vmem((4, gran, rows), F32),
+            dma((8,)), dma((2,)), dma((8,)), dma((8,)), dma((4,)), dma((4,)), dma((4,)), dma((4,)), dma((8,)), dma((8,)),
+            dma((7,)), dma((7,)), dma((7,)), dma((7,)), dma((7,)), dma((7,)),
         ],
         compiler_params=pltpu.CompilerParams(
-            collective_id=0, has_side_effects=True, vmem_limit_bytes=48 * 1024 * 1024
+            collective_id=0, has_side_effects=True, vmem_limit_bytes=60 * 1024 * 1024
         ),
-        cost_estimate=pl.CostEstimate(flops=flops, bytes_accessed=5 * 1024 * 1024, transcendentals=0),
+        cost_estimate=pl.CostEstimate(flops=4 * n * n * n, bytes_accessed=5 * 1024 * 1024, transcendentals=0),
     )(integrals, density, tile_mask)
 
 

time: 91 us -> 76.6 us (0.84)
  Pallas kernels: 86.9 us -> 74.3 us
  local copies, waits for them, and re-layouts: 3.88 us -> 1.57 us
    pallas_call x1, Pallas kernels: 86.9 us -> 74.3 us  [fused(): pl.pallas_call(exchange_kernel, out_shape=jax.ShapeDtypeStruct((gran, n),...]
    unnamed x7 -> x1, local copies, waits for them, and re-layouts: 3.88 us -> 1.57 us
where the time goes in v2:
time: 76.6 us; the launch traced here: 75.9 us
  Pallas kernels  74.3 us (97%)
  local copies, waits for them, and re-layouts  1.57 us (2%)
    pallas_call x1, Pallas kernels, fused(): pl.pallas_call(exchange_kernel, out_shape=jax.ShapeDtypeStruct((gran, n),...  74.3 us
    unnamed x1, local copies, waits for them, and re-layouts  1.57 us

profile of v2, /device:TPU:0, one launch (start us, length us, event | category | flops | bytes accessed | tf_op | source)
XLA Modules:
  0.0 75.9 jit_solution(7466606887901648344)
XLA Ops:
  0.0 74.3 %shard_map.37 = bf16[64,1024]{1,0:T(8,128)(2,1)} custom-call(bf16[8,256,512]{2,1,0:T(8,128)(2,1)} %x_hbm.1, bf16[128,1024]{1,0:T(8,128)(2,1)} %d_hbm.1, s32[1,4,8]{2,1,0:T(4,128)} %mask_ref.1), custom_call_target="tpu_custom_call" | custom-call | flops 4294967296 | bytes 5242880 | tf_op jit(solution)/shard_map/pallas_call | solution.py:240
  74.3 1.6 %copy.5 = bf16[64,1024]{1,0:T(8,128)(2,1)} copy(bf16[64,1024]{1,0:T(8,128)(2,1)} %shard_map.37) | data formatting | bytes 262144

commit v3 on v2

--- a/solution.py
+++ b/solution.py
@@ -11,11 +11,10 @@
 BF16 = jnp.bfloat16
 A2A_ORDER = ((2, 0), (2, 1), (1, 0), (0, 1), (1, 1), (3, 0), (3, 1))
 FIRST, SECOND = 2, 5
-ZFIRST = False
 
 
 EARLY = ((2, 0, 3), (1, 0, 3), (0, 0, 3))
-LATE = ((3, 0, 4), (2, 3, 1), (1, 3, 1), (0, 3, 1))
+LATE = ((3, 0, 2), (3, 2, 2), (2, 3, 1), (1, 3, 1), (0, 3, 1))
 
 
 def exchange_kernel(
@@ -156,10 +155,12 @@
                 kf[k, q2, j, c2] = part
                 ks[k, q2, j, c2] = part.astype(BF16)
 
-    def row_block(k):
+    def landed(k):
         for cc in ((1,) if k == 0 else (0, 1)):
             b = blocks[(k, cc)]
             arrive(owned.at[b], a_send.at[b], a_recv.at[b])
+
+    def half_block(k):
         for s in range(0, n, 256):
             acc = jnp.zeros((rows, 256), F32)
             for cc in range(2):
@@ -192,7 +193,8 @@
             tot[js] = total
 
     for k in range(3):
-        row_block(k)
+        landed(k)
+        half_block(k)
         for j in range(k):
             product(k, j)
             product(j, k)
@@ -201,19 +203,16 @@
         over_core(item)
     for item in EARLY:
         over_x(item)
-    if ZFIRST:
-        for item in EARLY:
-            over_z(item)
-    row_block(3)
-    for j in range(4):
-        product(3, j)
-    over_core(LATE[0])
-    for k in (2, 1, 0):
-        product(k, 3)
-        over_core(LATE[3 - k])
-    if not ZFIRST:
-        for item in EARLY:
-            over_z(item)
+    landed(3)
+    over_z(EARLY[0])
+    half_block(3)
+    for item in LATE:
+        k, j, size = item
+        for at in range(j, j + size):
+            product(k, at)
+        over_core(item)
+    for item in EARLY[1:]:
+        over_z(item)
     for item in LATE:
         over_x(item)
     for item in LATE:
@@ -260,7 +259,7 @@
             vmem((4, 4, gran, rows), BF16),
             vmem((4, gran, rows), F32),
             dma((8,)), dma((2,)), dma((8,)), dma((8,)), dma((4,)), dma((4,)), dma((4,)), dma((4,)), dma((8,)), dma((8,)),
-            dma((7,)), dma((7,)), dma((7,)), dma((7,)), dma((7,)), dma((7,)),
+            dma((len(EARLY + LATE),)), dma((len(EARLY + LATE),)), dma((len(EARLY + LATE),)), dma((len(EARLY + LATE),)), dma((len(EARLY + LATE),)), dma((len(EARLY + LATE),)),
         ],
         compiler_params=pltpu.CompilerParams(
             collective_id=0, has_side_effects=True, vmem_limit_bytes=60 * 1024 * 1024

time: 76.6 us -> 76.2 us (level)
  no operation moved by 1% of the time
where the time goes in v3:
time: 76.2 us; the launch traced here: 76 us
  Pallas kernels  74.4 us (98%)
  local copies, waits for them, and re-layouts  1.57 us (2%)
    pallas_call x1, Pallas kernels, fused(): pl.pallas_call(exchange_kernel, out_shape=jax.ShapeDtypeStruct((gran, n),...  74.4 us
    unnamed x1, local copies, waits for them, and re-layouts  1.57 us

profile of v3, /device:TPU:0, one launch (start us, length us, event | category | flops | bytes accessed | tf_op | source)
XLA Modules:
  0.0 76.0 jit_solution(12633527942225510228)
XLA Ops:
  0.0 74.4 %shard_map.37 = bf16[64,1024]{1,0:T(8,128)(2,1)} custom-call(bf16[8,256,512]{2,1,0:T(8,128)(2,1)} %x_hbm.1, bf16[128,1024]{1,0:T(8,128)(2,1)} %d_hbm.1, s32[1,4,8]{2,1,0:T(4,128)} %mask_ref.1), custom_call_target="tpu_custom_call" | custom-call | flops 4294967296 | bytes 5242880 | tf_op jit(solution)/shard_map/pallas_call | solution.py:239
  74.4 1.6 %copy.5 = bf16[64,1024]{1,0:T(8,128)(2,1)} copy(bf16[64,1024]{1,0:T(8,128)(2,1)} %shard_map.37) | data formatting | bytes 262144
